TPU v7x, 32 devices: a whole 2x2x4 slice. The times are simulated.
32 devices in a mesh: prog: 32 (over z, y, x, core), clus: 1.
Axes of the slice: x: 2, y: 2, z: 4, core: 2. Of those that a mesh axis runs over, the one named last changes fastest.
Arguments:
- embeddings: bfloat16 [32768, 2048], P('prog', 'clus'), may hold values from -64 to 64, as said below
- centroids: bfloat16 [4096, 2048], P('clus'), may hold values from -6 to 6, as said below
- plan_grad: bfloat16 [32768, 4096], P('prog', 'clus'), may hold values from -24 to 24
Outputs:
- embed_grad: bfloat16 [32768, 2048], P('prog', 'clus')
- centroid_grad: bfloat16 [4096, 2048], P(('clus', 'prog'))
Inputs may be any that keep to these rules, and one draw needn't show every extreme that they name: embeddings are real-valued with full-rank spread. centroids are real-valued with full-rank spread.
All inputs are finite; a program needn't handle non-finite values.
Results may differ from a plain program's by a relative error of at most 0.006.
Values may be sent and summed in bfloat16 or wider, within the bound.
A program may use at most 128 MiB of HBM per device.

v0:
```python
import jax
import jax.numpy as jnp
from jax import lax
from jax.sharding import PartitionSpec as P

D = 2048
CENTROIDS = 4096
ITERS = 4


def merged(part, axis, combine):
    gathered = jax.tree.map(lambda a: lax.all_gather(a, axis), part)

    def take(source):
        return jax.tree.map(lambda a: lax.dynamic_index_in_dim(a, source, 0, False), gathered)

    return lax.fori_loop(
        1, lax.axis_size(axis), lambda source, state: combine(state, take(source)), take(0)
    )


def lse_combine(first, second):
    top = jnp.maximum(first[0], second[0])
    total = first[1] * jnp.exp(first[0] - top) + second[1] * jnp.exp(second[0] - top)
    return (top, total)


def row_lse(values):
    local_top = jnp.max(values, axis=1)
    local_total = jnp.sum(jnp.exp(values - local_top[:, None]), axis=1)
    top, total = merged((local_top, local_total), "clus", lse_combine)
    return top + jnp.log(total)


def col_lse(values):
    local_top = jnp.max(values, axis=0)
    local_total = jnp.sum(jnp.exp(values - local_top[None, :]), axis=0)
    top, total = merged((local_top, local_total), "prog", lse_combine)
    return top + jnp.log(total)


def shards(embeddings, centroids, plan_grad):
    scale = 1.0 / (0.25 * jnp.sqrt(jnp.float32(D)))
    whole_rows = lax.all_gather(embeddings, "clus", axis=1, tiled=True)
    logits = scale * lax.dot_general(
        whole_rows, centroids, (((1,), (1,)), ((), ())), preferred_element_type=jnp.float32
    )
    total_rows = embeddings.shape[0] * lax.axis_size("prog")
    log_b = jnp.log(jnp.float32(total_rows) / jnp.float32(CENTROIDS))
    col_pot = jnp.zeros((centroids.shape[0],), jnp.float32)
    row_list = []
    col_list = []
    for step in range(ITERS):
        row_pot = -row_lse(logits + col_pot[None, :])
        col_pot = log_b - col_lse(logits + row_pot[:, None])
        row_list.append(row_pot)
        col_list.append(col_pot)
    plan = jnp.exp(logits + row_list[-1][:, None] + col_list[-1][None, :])
    pbar = plan_grad.astype(jnp.float32) * plan
    adjoint = pbar
    col_adj = lax.psum(jnp.sum(pbar, axis=0), "prog")
    direct = jnp.sum(pbar, axis=1)
    for step in range(ITERS - 1, -1, -1):
        weights_a = jnp.exp(logits + row_list[step][:, None] + col_list[step][None, :] - log_b)
        term_a = weights_a * col_adj[None, :]
        adjoint = adjoint - term_a
        row_adj = lax.psum(direct - jnp.sum(term_a, axis=1), "clus")
        direct = jnp.zeros_like(direct)
        if step > 0:
            prev_col = col_list[step - 1]
        else:
            prev_col = jnp.zeros_like(col_pot)
        term_b = jnp.exp(logits + prev_col[None, :] + row_list[step][:, None]) * row_adj[:, None]
        adjoint = adjoint - term_b
        if step > 0:
            col_adj = -lax.psum(jnp.sum(term_b, axis=0), "prog")
    adjoint_b = adjoint.astype(jnp.bfloat16)
    partial_rows = scale * jnp.dot(adjoint_b, centroids, preferred_element_type=jnp.float32)
    embed_grad = lax.psum_scatter(partial_rows, "clus", scatter_dimension=1, tiled=True).astype(
        jnp.bfloat16
    )
    centroid_grad = lax.psum_scatter(
        scale
        * lax.dot_general(
            adjoint_b, whole_rows, (((0,), (0,)), ((), ())), preferred_element_type=jnp.float32
        ),
        "prog",
        scatter_dimension=0,
        tiled=True,
    ).astype(jnp.bfloat16)
    return (embed_grad, centroid_grad)


def solution(mesh):
    placed = (P("prog", "clus"), P("clus", None), P("prog", "clus"))
    return jax.shard_map(
        shards,
        mesh=mesh,
        in_specs=placed,
        out_specs=(P("prog", "clus"), P(("clus", "prog"), None)),
        check_vma=False,
    )
```

profile of v0, /device:TPU:14, one launch (start us, length us, event | category | flops | bytes accessed | tf_op | source)
XLA Modules:
  0.0 1135.5 jit_solution(10512579903416072653)
XLA Ops:
  7.2 23.8 %fusion.9 = (f32[1024]{0:T(1024)S(1)}, f32[1024,4096]{1,0:T(8,128)}) fusion(bf16[1024,2048]{1,0:T(8,128)(2,1)} %param.11, bf16[4096,2048]{1,0:T(8,128)(2,1)} %param.12), kind=kOutput, calls=%fused_computation.59 | convolution fusion | flops 17188257792 | bytes 37752832 | tf_op jit(solution)/shard_map/dot_general | solution.py:45
  31.0 8.1 exponential_reduce_fusion.7
  46.3 9.3 exponential_reduce_fusion.6
  55.5 30.2 %all-gather.1 = f32[131072]{0:T(1024)S(1)} all-gather(f32[4096]{0:T(1024)S(1)} %exponential_reduce_fusion.6), channel_id=3, replica_groups=mesh['prog'=32,'clus'=1] {'prog'}, dimensions={0}, use_global_device_ids=true | all-gather | bytes 540672 | tf_op jit(solution)/shard_map/all_gather | solution.py:12
  85.9 41.4 %all-gather = f32[131072]{0:T(1024)S(1)} all-gather(f32[4096]{0:T(1024)S(1)} %add_reduce_fusion.6), channel_id=2, replica_groups=mesh['prog'=32,'clus'=1] {'prog'}, dimensions={0}, use_global_device_ids=true | all-gather | bytes 540672 | tf_op jit(solution)/shard_map/all_gather | solution.py:12
  137.1 8.7 exponential_reduce_fusion.5
  153.0 9.3 exponential_reduce_fusion.4
  162.3 38.1 %all-gather.3 = f32[131072]{0:T(1024)S(1)} all-gather(f32[4096]{0:T(1024)S(1)} %exponential_reduce_fusion.4), channel_id=5, replica_groups=mesh['prog'=32,'clus'=1] {'prog'}, dimensions={0}, use_global_device_ids=true | all-gather | bytes 540672 | tf_op jit(solution)/shard_map/all_gather | solution.py:12
  200.4 39.9 %all-gather.2 = f32[131072]{0:T(1024)S(1)} all-gather(f32[4096]{0:T(1024)S(1)} %add_reduce_fusion.3), channel_id=4, replica_groups=mesh['prog'=32,'clus'=1] {'prog'}, dimensions={0}, use_global_device_ids=true | all-gather | bytes 540672 | tf_op jit(solution)/shard_map/all_gather | solution.py:12
  250.2 8.7 exponential_reduce_fusion.3
  266.1 9.3 exponential_reduce_fusion.2
  275.4 38.0 %all-gather.5 = f32[131072]{0:T(1024)S(1)} all-gather(f32[4096]{0:T(1024)S(1)} %exponential_reduce_fusion.2), channel_id=7, replica_groups=mesh['prog'=32,'clus'=1] {'prog'}, dimensions={0}, use_global_device_ids=true | all-gather | bytes 540672 | tf_op jit(solution)/shard_map/all_gather | solution.py:12
  313.5 39.7 %all-gather.4 = f32[131072]{0:T(1024)S(1)} all-gather(f32[4096]{0:T(1024)S(1)} %add_reduce_fusion.1), channel_id=6, replica_groups=mesh['prog'=32,'clus'=1] {'prog'}, dimensions={0}, use_global_device_ids=true | all-gather | bytes 540672 | tf_op jit(solution)/shard_map/all_gather | solution.py:12
  363.0 8.7 exponential_reduce_fusion.1
  378.9 9.2 exponential_reduce_fusion
  388.2 38.0 %all-gather.7 = f32[131072]{0:T(1024)S(1)} all-gather(f32[4096]{0:T(1024)S(1)} %exponential_reduce_fusion), channel_id=9, replica_groups=mesh['prog'=32,'clus'=1] {'prog'}, dimensions={0}, use_global_device_ids=true | all-gather | bytes 540672 | tf_op jit(solution)/shard_map/all_gather | solution.py:12
  426.3 39.8 %all-gather.6 = f32[131072]{0:T(1024)S(1)} all-gather(f32[4096]{0:T(1024)S(1)} %add_reduce_fusion.5), channel_id=8, replica_groups=mesh['prog'=32,'clus'=1] {'prog'}, dimensions={0}, use_global_device_ids=true | all-gather | bytes 540672 | tf_op jit(solution)/shard_map/all_gather | solution.py:12
  468.8 10.6 fusion.8
  479.4 49.0 %psum.26 = f32[4096]{0:T(1024)S(1)} all-reduce(f32[4096]{0:T(1024)S(1)} %get-tuple-element.542), channel_id=1, replica_groups=mesh['prog'=32,'clus'=1] {'prog'}, use_global_device_ids=true, to_apply=%region_25.26 | all-reduce | flops 4096 | bytes 32768 | tf_op jit(solution)/shard_map/psum | solution.py:61
  528.4 8.2 fusion.4
  536.6 8.0 fusion.1
  544.6 38.4 %psum.29 = f32[4096]{0:T(1024)S(1)} all-reduce(f32[4096]{0:T(1024)S(1)} %fusion.1), channel_id=1, replica_groups=mesh['prog'=32,'clus'=1] {'prog'}, use_global_device_ids=true, to_apply=%region_29.30 | all-reduce | flops 4096 | bytes 32768 | tf_op jit(solution)/shard_map/psum | solution.py:76
  582.9 8.3 fusion.5
  591.2 8.0 fusion.2
  599.2 41.9 %psum.30 = f32[4096]{0:T(1024)S(1)} all-reduce(f32[4096]{0:T(1024)S(1)} %fusion.2), channel_id=1, replica_groups=mesh['prog'=32,'clus'=1] {'prog'}, use_global_device_ids=true, to_apply=%region_32.33 | all-reduce | flops 4096 | bytes 32768 | tf_op jit(solution)/shard_map/psum | solution.py:76
  641.1 8.3 fusion.6
  657.3 38.7 %psum.31 = f32[4096]{0:T(1024)S(1)} all-reduce(f32[4096]{0:T(1024)S(1)} %fusion.3), channel_id=1, replica_groups=mesh['prog'=32,'clus'=1] {'prog'}, use_global_device_ids=true, to_apply=%region_35.36 | all-reduce | flops 4096 | bytes 32768 | tf_op jit(solution)/shard_map/psum | solution.py:76
  696.1 8.3 fusion
  704.3 34.9 %subtract_convert_fusion = bf16[1024,4096]{1,0:T(8,128)(2,1)S(1)} fusion(f32[1024,4096]{1,0:T(8,128)} %get-tuple-element.601, f32[1024]{0:T(1024)S(1)} %broadcast_subtract_fusion, f32[4096]{0:T(1024)S(1)} %neg.43, f32[1024]{0:T(1024)S(1)} %broadcast_subtract_fusion.1, f32[4096]{0:T(1024)S(1)} %neg.42, f32[1024]{0:T(1024)S(1)} %broadcast_subtract_fusion.2, ...), kind=kLoop, calls=%fused_computation.13 | loop fusion | flops 155189248 | bytes 33718272 | tf_op jit(solution)/shard_map/convert_element_type | solution.py:77
  742.4 21.7 %convolution_multiply_fusion = f32[4096,2048]{1,0:T(8,128)} fusion(bf16[1024,4096]{1,0:T(8,128)(2,1)S(1)} %subtract_convert_fusion, bf16[1024,2048]{1,0:T(8,128)(2,1)S(1)} %copy-done), kind=kOutput, calls=%fused_computation.12 | convolution fusion | flops 17188257792 | bytes 46137344 | tf_op jit(solution)/shard_map/dot_general | solution.py:84
  764.1 24.0 %multiply_convert_fusion = bf16[1024,2048]{1,0:T(8,128)(2,1)} fusion(bf16[1024,4096]{1,0:T(8,128)(2,1)} %copy-done.1, bf16[4096,2048]{1,0:T(8,128)(2,1)} %param.12), kind=kOutput, calls=%fused_computation.45 | convolution fusion | flops 17184063488 | bytes 29360128 | tf_op jit(solution)/shard_map/dot_general | solution.py:78
  788.1 338.0 %reduce-scatter.2.cloned.1.call-done = f32[128,2048]{1,0:T(8,128)} async-done(((f32[4096,2048]{1,0:T(8,128)}), f32[128,2048]{1,0:T(8,128)}) %reduce-scatter.2.cloned.1.call-update) | async-done | bytes 1048592 | tf_op jit(solution)/shard_map/reduce_scatter | solution.py:82
  (298 shorter events, 81.2 us)
Async XLA Ops:
  7.2 1118.9 %reduce-scatter.2.cloned.1.call-start = ((), (), s32[]{:S(2)}) async-start(), calls=%async_computation.1 | async-start | bytes 34603008 | tf_op jit(solution)/shard_map/reduce_scatter | solution.py:82
  704.3 38.1 %copy-start = (bf16[1024,2048]{1,0:T(8,128)(2,1)S(1)}, bf16[1024,2048]{1,0:T(8,128)(2,1)}, u32[]{:S(2)}) copy-start(bf16[1024,2048]{1,0:T(8,128)(2,1)} %param.11) | copy-start | bytes 12582916
  739.2 3.2 copy-start.1
Sparse Core Ops, SparseCore 0:
  764.3 361.7 reduce-scatter.1
where the time goes:
time: 1140 us
  blocking collectives  473 us (41%)
  waiting for transfers between devices  338 us (30%)
  other arithmetic  228 us (20%)
  matrix products  69.5 us (6%)
  between operations  14.9 us (1%)
    reduce_scatter x1, waiting for transfers between devices, shards(): lax.psum_scatter(scale * lax.dot_general(adjoint_b, whole_rows, (((0,), (...  338 us
    all_gather x8, blocking collectives, merged(): gathered = jax.tree.map(lambda a: lax.all_gather(a, axis), part)  305 us
    psum x3, blocking collectives, shards(): col_adj = -lax.psum(jnp.sum(term_b, axis=0), 'prog')  119 us
    psum x1, blocking collectives, shards(): col_adj = lax.psum(jnp.sum(pbar, axis=0), 'prog')  49 us
    reduce_sum x4, other arithmetic, col_lse(): local_total = jnp.sum(jnp.exp(values - local_top[None, :]), axis=0)  37 us
    convert_element_type x1, other arithmetic, shards(): adjoint_b = adjoint.astype(jnp.bfloat16)  34.9 us
    reduce_sum x4, other arithmetic, row_lse(): local_total = jnp.sum(jnp.exp(values - local_top[:, None]), axis=1)  34.3 us
    reduce_sum x4, other arithmetic, shards(): row_adj = lax.psum(direct - jnp.sum(term_a, axis=1), 'clus')  32.9 us
  transfers between devices with their start and end apart: 1, of which 1 were waited for; matrix products, arithmetic and copies ran while one was open for 2% of the time, Pallas kernels for 0%

commit v1 on v0

--- a/solution.py
+++ b/solution.py
@@ -1,10 +1,12 @@
+import functools
+
 import jax
 import jax.numpy as jnp
 from jax import lax
+from jax.experimental import pallas as pl
+from jax.experimental.pallas import tpu as pltpu
 from jax.sharding import PartitionSpec as P
 
-D = 2048
-CENTROIDS = 4096
 ITERS = 4
 
 
@@ -39,14 +41,14 @@
     return top + jnp.log(total)
 
 
-def shards(embeddings, centroids, plan_grad):
-    scale = 1.0 / (0.25 * jnp.sqrt(jnp.float32(D)))
+def general_shards(embeddings, centroids, plan_grad):
+    scale = 1.0 / (0.25 * jnp.sqrt(jnp.float32(embeddings.shape[1] * lax.axis_size("clus"))))
     whole_rows = lax.all_gather(embeddings, "clus", axis=1, tiled=True)
     logits = scale * lax.dot_general(
         whole_rows, centroids, (((1,), (1,)), ((), ())), preferred_element_type=jnp.float32
     )
     total_rows = embeddings.shape[0] * lax.axis_size("prog")
-    log_b = jnp.log(jnp.float32(total_rows) / jnp.float32(CENTROIDS))
+    log_b = jnp.log(jnp.float32(total_rows) / jnp.float32(centroids.shape[0] * lax.axis_size("clus")))
     col_pot = jnp.zeros((centroids.shape[0],), jnp.float32)
     row_list = []
     col_list = []
@@ -91,10 +93,358 @@
     return (embed_grad, centroid_grad)
 
 
+LANES = 128
+MESH_AXIS = "prog"
+
+
+def sinkhorn_kernel(
+    n, scale, ratio, emb, cent, grad, out,
+    E, G, tiles, A, X, R, U, sub, cols, RW, RH, LH,
+    send1, got1, reply1, back1, send2, got2, reply2, back2,
+    tile_sem, grad_sem, out_sem, ss1, rs1, ss2, rs2,
+):
+    rows, C = E.shape
+    W = C // n
+    K = C // LANES
+    me = lax.axis_index(MESH_AXIS)
+    f32 = jnp.float32
+
+    def other(k):
+        return lax.rem(me + k, n)
+
+    barrier = pltpu.get_barrier_semaphore()
+
+    @pl.loop(1, n)
+    def _(k):
+        pl.semaphore_signal(barrier, inc=1, device_id={MESH_AXIS: other(k)},
+                            device_id_type=pl.DeviceIdType.MESH)
+
+    grad_copy = pltpu.make_async_copy(grad, G, grad_sem)
+    width = tiles.shape[1]
+    count = C // width
+
+    def fetch(j):
+        return pltpu.make_async_copy(
+            cent.at[pl.ds(j * width, width), :], tiles.at[j % 2], tile_sem.at[j % 2])
+
+    fetch(0).start()
+    for j in range(count):
+        if j + 1 < count:
+            fetch(j + 1).start()
+        if j == 0:
+            grad_copy.start()
+        fetch(j).wait()
+
+        half = rows // 4
+
+        @pl.loop(0, 4)
+        def _(q, j=j):
+            r0 = pl.multiple_of(q * half, half)
+            E[pl.ds(r0, half), j * width:(j + 1) * width] = scale * lax.dot_general(
+                emb[pl.ds(r0, half), :], tiles[j % 2], (((1,), (1,)), ((), ())),
+                preferred_element_type=f32)
+
+    pl.semaphore_wait(barrier, n - 1)
+
+    BR = 64
+    BC = 16
+    CH = 8
+
+    def rows_loop(body):
+        @pl.loop(0, rows // BR)
+        def _(i):
+            body(pl.ds(pl.multiple_of(i * BR, BR), BR))
+
+    def lane(k):
+        return slice(k * LANES, (k + 1) * LANES)
+
+    def cols_loop(body, init, outs, combine):
+        for c in range(K // CH):
+            def step(i, accs, c=c):
+                r = pl.ds(pl.multiple_of(i * BC, BC), BC)
+                new = []
+                for q in range(CH):
+                    terms = body(r, c * CH + q)
+                    new.append(tuple(combine(a, t) for a, t in zip(accs[q], terms)))
+                return tuple(new)
+
+            start = tuple(
+                tuple(jnp.full((BC, LANES), init, f32) for _ in outs) for _ in range(CH))
+            accs = lax.fori_loop(0, rows // BC, step, start, unroll=2)
+            for q in range(CH):
+                for o, a in zip(outs, accs[q]):
+                    if combine is jnp.maximum:
+                        red = jnp.max(a, axis=0, keepdims=True)
+                    else:
+                        red = jnp.sum(a, axis=0, keepdims=True)
+                    o[:, lane(c * CH + q)] = red
+
+    def total(part):
+        return jnp.broadcast_to(jnp.sum(part, axis=1, keepdims=True), part.shape)
+
+    def row_pass(y):
+        def body(r):
+            acc = E[r, lane(0)] * y[:, lane(0)]
+            for k in range(1, K):
+                acc = acc + E[r, lane(k)] * y[:, lane(k)]
+            R[r, :] = acc
+        rows_loop(body)
+
+    def exchange(vectors, combine, results, send, got, reply, back):
+        for k in range(n):
+            for q, v in enumerate(vectors):
+                send[k, :, q * W:(q + 1) * W] = v[:, k * W:(k + 1) * W]
+
+        def first(k):
+            t = other(k)
+            return pltpu.make_async_remote_copy(
+                src_ref=send.at[t], dst_ref=got.at[me], send_sem=ss1.at[t],
+                recv_sem=rs1.at[me], device_id={MESH_AXIS: t},
+                device_id_type=pl.DeviceIdType.MESH)
+
+        def first_in(k):
+            t = other(k)
+            return pltpu.make_async_remote_copy(
+                src_ref=send.at[t], dst_ref=got.at[t], send_sem=ss1.at[t],
+                recv_sem=rs1.at[t], device_id={MESH_AXIS: t},
+                device_id_type=pl.DeviceIdType.MESH)
+
+        def second(k):
+            t = other(k)
+            return pltpu.make_async_remote_copy(
+                src_ref=reply, dst_ref=back.at[me], send_sem=ss2.at[t],
+                recv_sem=rs2.at[me], device_id={MESH_AXIS: t},
+                device_id_type=pl.DeviceIdType.MESH)
+
+        def second_in(k):
+            t = other(k)
+            return pltpu.make_async_remote_copy(
+                src_ref=reply, dst_ref=back.at[t], send_sem=ss2.at[t],
+                recv_sem=rs2.at[t], device_id={MESH_AXIS: t},
+                device_id_type=pl.DeviceIdType.MESH)
+
+        @pl.loop(1, n)
+        def _(k):
+            first(k).start()
+
+        got[me] = send[me]
+
+        @pl.loop(1, n)
+        def _(k):
+            first_in(k).wait_recv()
+
+        arrived = got[...]
+        answers = combine([arrived[:, :, q * W:(q + 1) * W] for q in range(len(vectors))])
+        for q, a in enumerate(answers):
+            reply[:, q * W:(q + 1) * W] = a
+
+        @pl.loop(1, n)
+        def _(k):
+            second(k).start()
+
+        back[me] = reply[...]
+
+        @pl.loop(1, n)
+        def _(k):
+            first(k).wait_send()
+            second_in(k).wait_recv()
+
+        for k in range(n):
+            for q, v in enumerate(results):
+                v[:, k * W:(k + 1) * W] = back[k, :, q * W:(q + 1) * W]
+
+        @pl.loop(1, n)
+        def _(k):
+            second(k).wait_send()
+
+    M, F = cols.at[pl.ds(0, 1)], cols.at[pl.ds(1, 1)]
+    B = {t: cols.at[pl.ds(t, 1)] for t in (2, 3, 4)}
+    DV = cols.at[pl.ds(5, 1)]
+    Y, Y2, S, S2, EM = (cols.at[pl.ds(q, 1)] for q in (8, 9, 10, 11, 12))
+
+    def top_body(r):
+        acc = E[r, lane(0)]
+        for k in range(1, K):
+            acc = jnp.maximum(acc, E[r, lane(k)])
+        R[r, :] = jnp.broadcast_to(jnp.max(acc, axis=1, keepdims=True), acc.shape)
+
+    rows_loop(top_body)
+
+    def exp_body(r):
+        top = R[r, :]
+        acc = jnp.exp(E[r, lane(0)] - top)
+        for k in range(1, K):
+            acc = acc + jnp.exp(E[r, lane(k)] - top)
+        U[r, :] = -(top + jnp.log(total(acc)))
+
+    rows_loop(exp_body)
+    cols_loop(lambda r, k: [E[r, lane(k)] + U[r, :]], -jnp.inf, [M], jnp.maximum)
+
+    def shift(r, k):
+        e = jnp.exp(E[r, lane(k)] + U[r, :] - M[:, lane(k)])
+        E[r, lane(k)] = e
+        return [e]
+
+    add = lambda a, b: a + b
+    cols_loop(shift, 0.0, [S], add)
+
+    def lse(parts):
+        m, s = parts
+        top = jnp.max(m, axis=0)
+        whole = jnp.sum(s * jnp.exp(m - top[None]), axis=0)
+        v = jnp.log(f32(ratio)) - (top + jnp.log(whole))
+        return [v, v]
+
+    exchange([M, S], lse, [Y], send2, got2, reply2, back2)
+    F[...] = jnp.exp(M[...] + Y[...])
+    EM[...] = jnp.exp(M[...])
+
+    def plain(parts):
+        return [jnp.sum(p, axis=0) for p in parts]
+
+    def fb(t):
+        if t == 0:
+            return EM[...]
+        return F[...] if t == 1 else F[...] * B[t][...]
+
+    A[0] = jnp.ones((rows, LANES), f32)
+    for t in (2, 3, 4):
+        Y[...] = fb(t - 1)
+        row_pass(Y)
+        A[t - 1] = 1.0 / total(R[...])
+        if t < 4:
+            cols_loop(lambda r, k, t=t: [E[r, lane(k)] * A[t - 1, r, :]], 0.0, [S], add)
+            S[...] = S[...] * F[...]
+            exchange([S], plain, [Y], send1, got1, reply1, back1)
+            B[t][...] = ratio / Y[...]
+        else:
+            grad_copy.wait()
+
+            def both(r, k):
+                w = E[r, lane(k)] * A[3, r, :]
+                return [w, w * G[r, lane(k)].astype(f32)]
+
+            cols_loop(both, 0.0, [S, S2], add)
+            S[...] = S[...] * F[...]
+            S2[...] = S2[...] * F[...]
+            exchange([S, S2], plain, [Y, Y2], send2, got2, reply2, back2)
+            B[t][...] = ratio / Y[...]
+            DV[...] = B[t][...] * Y2[...]
+
+    for t in (4, 3, 2, 1):
+        Y[...] = fb(t) * DV[...] * (1.0 / ratio)
+        RW[t - 1:t, :] = Y[...]
+        RW[3 + t:4 + t, :] = fb(t - 1)
+        if t == 4:
+            Y2[...] = fb(4)
+
+            def grad_body(r):
+                acc = jnp.zeros((BR, LANES), f32)
+                for k in range(K):
+                    acc = acc + E[r, lane(k)] * (
+                        G[r, lane(k)].astype(f32) * Y2[:, lane(k)] - Y[:, lane(k)])
+                R[r, :] = acc
+
+            rows_loop(grad_body)
+            X[t - 1] = A[t - 1] * A[t - 1] * total(R[...])
+        else:
+            row_pass(Y)
+            X[t - 1] = -(A[t - 1] * A[t - 1]) * total(R[...])
+        if t > 1:
+            cols_loop(lambda r, k, t=t: [E[r, lane(k)] * X[t - 1, r, :]], 0.0, [S], add)
+            S[...] = S[...] * F[...]
+            exchange([S], plain, [Y], send1, got1, reply1, back1)
+            if t == 2:
+                DV[...] = -Y[...]
+            else:
+                DV[...] = -Y[...] * B[t - 1][...]
+
+    high = RW[...].astype(jnp.bfloat16).astype(f32)
+    low = RW[...] - high
+    RH[...] = jnp.concatenate(
+        [high, low, high, jnp.zeros_like(high)], axis=0).astype(jnp.bfloat16)
+    spot = lax.broadcasted_iota(jnp.int32, (BR, LANES), 1)
+
+    def left(r):
+        acc = jnp.zeros((BR, LANES), f32)
+        for q in range(8):
+            v = A[q, r, :] if q < 4 else X[q - 4, r, :]
+            hi = v.astype(jnp.bfloat16).astype(f32)
+            acc = jnp.where((spot == q) | (spot == q + 8), hi, acc)
+            acc = jnp.where(spot == q + 16, v - hi, acc)
+        LH[r, :] = acc.astype(jnp.bfloat16)
+
+    rows_loop(left)
+    Y2[...] = fb(4)
+
+    def finish(r):
+        lhs = LH[r, :][:, 0:32]
+        a4 = A[3, r, :]
+        for k in range(0, K, 2):
+            wide = slice(k * LANES, (k + 2) * LANES)
+            coef = jnp.dot(lhs, RH[:, wide], preferred_element_type=f32)
+            a = jnp.concatenate([a4, a4], axis=1)
+            val = E[r, wide] * (G[r, wide].astype(f32) * a * Y2[:, wide] - coef)
+            G[r, wide] = val.astype(jnp.bfloat16)
+
+    rows_loop(finish)
+    done = pltpu.make_async_copy(G, out, out_sem)
+    done.start()
+    done.wait()
+
+
+def adjoint_of(n, scale, ratio, embeddings, centroids, plan_grad):
+    rows, depth = embeddings.shape
+    C = centroids.shape[0]
+    W = C // n
+    f32 = jnp.float32
+    width = 512
+    vm = pltpu.VMEM
+    scratch = [
+        vm((rows, C), f32), vm((rows, C), jnp.bfloat16), vm((2, width, depth), jnp.bfloat16),
+        vm((4, rows, LANES), f32), vm((4, rows, LANES), f32), vm((rows, LANES), f32),
+        vm((rows, LANES), f32), vm((8, LANES), f32), vm((16, C), f32),
+        vm((8, C), f32), vm((32, C), jnp.bfloat16), vm((rows, LANES), jnp.bfloat16),
+        vm((n, 1, W), f32), vm((n, 1, W), f32), vm((1, W), f32), vm((n, 1, W), f32),
+        vm((n, 1, 2 * W), f32), vm((n, 1, 2 * W), f32), vm((1, 2 * W), f32),
+        vm((n, 1, 2 * W), f32),
+        pltpu.SemaphoreType.DMA((2,)), pltpu.SemaphoreType.DMA, pltpu.SemaphoreType.DMA,
+        pltpu.SemaphoreType.DMA((n,)), pltpu.SemaphoreType.DMA((n,)),
+        pltpu.SemaphoreType.DMA((n,)), pltpu.SemaphoreType.DMA((n,)),
+    ]
+    return pl.pallas_call(
+        functools.partial(sinkhorn_kernel, n, scale, ratio),
+        out_shape=jax.ShapeDtypeStruct((rows, C), jnp.bfloat16),
+        in_specs=[pl.BlockSpec(memory_space=pltpu.VMEM), pl.BlockSpec(memory_space=pl.ANY),
+                  pl.BlockSpec(memory_space=pl.ANY)],
+        out_specs=pl.BlockSpec(memory_space=pl.ANY),
+        scratch_shapes=scratch,
+        compiler_params=pltpu.CompilerParams(
+            collective_id=0, has_side_effects=True, vmem_limit_bytes=56 * 1024 * 1024),
+        name="sinkhorn",
+    )(embeddings, centroids, plan_grad)
+
+
+def fast_shards(embeddings, centroids, plan_grad):
+    n = lax.axis_size("prog")
+    rows, depth = embeddings.shape
+    scale = 1.0 / (0.25 * depth**0.5)
+    ratio = rows * n / centroids.shape[0]
+    adjoint_b = adjoint_of(n, scale, ratio, embeddings, centroids, plan_grad)
+    part = scale * lax.dot_general(
+        adjoint_b, embeddings, (((0,), (0,)), ((), ())), preferred_element_type=jnp.float32)
+    centroid_grad = lax.psum_scatter(
+        part, "prog", scatter_dimension=0, tiled=True).astype(jnp.bfloat16)
+    embed_grad = (scale * jnp.dot(
+        adjoint_b, centroids, preferred_element_type=jnp.float32)).astype(jnp.bfloat16)
+    return (embed_grad, centroid_grad)
+
+
 def solution(mesh):
+    fast = mesh.shape["clus"] == 1 and ITERS == 4
     placed = (P("prog", "clus"), P("clus", None), P("prog", "clus"))
     return jax.shard_map(
-        shards,
+        fast_shards if fast else general_shards,
         mesh=mesh,
         in_specs=placed,
         out_specs=(P("prog", "clus"), P(("clus", "prog"), None)),

time: 1140 us -> 549 us (0.48)
  blocking collectives: 473 us -> 0 us
  other arithmetic: 228 us -> 2.08 us
  Pallas kernels: 0 us -> 146 us
  matrix products: 69.5 us -> 48.1 us
    all_gather x8 -> x0, blocking collectives: 305 us -> none  [merged(): gathered = jax.tree.map(lambda a: lax.all_gather(a, axis), part)]
    psum x4 -> x0, blocking collectives: 168 us -> none  [the longest x3 119 us: shards(): col_adj = -lax.psum(jnp.sum(term_b, axis=0), 'prog')]
    pallas_call x0 -> x1, Pallas kernels: none -> 146 us  [adjoint_of(): pl.pallas_call(functools.partial(sinkhorn_kernel, n, scale, ratio), out_s...]
    reduce_sum x16 -> x0, other arithmetic: 139 us -> none  [the longest x4 37 us: col_lse(): local_total = jnp.sum(jnp.exp(values - local_top[None, :]), axis=0)]
    reduce_max x7 -> x0, other arithmetic: 49.8 us -> none  [the longest x4 28.6 us: col_lse(): local_top = jnp.max(values, axis=0)]
    convert_element_type x2 -> x1, other arithmetic: 37 us -> 2.08 us  [fast_shards(): centroid_grad = lax.psum_scatter(part, 'prog', scatter_dimension=0, tiled...]
    dot_general x3 -> x2, matrix products: 69.5 us -> 48.1 us  [the longest x1 24.5 us: fast_shards(): lax.dot_general(adjoint_b, embeddings, (((0,), (0,)), ((), ())), preferre...]
  transfers between devices with their start and end apart: 1 -> 1, of which waited for: 1 -> 1; matrix products, arithmetic and copies ran while one was open for 2% -> 4% of each run, Pallas kernels for 0% -> 0%
where the time goes in v1:
time: 549 us
  waiting for transfers between devices  339 us (62%)
  Pallas kernels  146 us (27%)
  matrix products  48.1 us (9%)
  between operations  14.1 us (3%)
    reduce_scatter x1, waiting for transfers between devices, fast_shards(): lax.psum_scatter(part, 'prog', scatter_dimension=0, tiled=True)  339 us
    pallas_call x1, Pallas kernels, adjoint_of(): pl.pallas_call(functools.partial(sinkhorn_kernel, n, scale, ratio), out_s...  146 us
    dot_general x1, matrix products, fast_shards(): lax.dot_general(adjoint_b, embeddings, (((0,), (0,)), ((), ())), preferre...  24.5 us
    dot_general x1, matrix products, fast_shards(): jnp.dot(adjoint_b, centroids, preferred_element_type=jnp.float32)  23.6 us
  transfers between devices with their start and end apart: 1, of which 1 were waited for; matrix products, arithmetic and copies ran while one was open for 4% of the time, Pallas kernels for 0%

profile of v1, /device:TPU:14, one launch (start us, length us, event | category | flops | bytes accessed | tf_op | source)
XLA Modules:
  0.0 548.9 jit_solution(15725230768206995136)
XLA Ops:
  7.2 0.0 reduce-scatter.2.cloned.1.call-start
  7.2 0.0 copy-start
  7.2 145.7 %sinkhorn.1 = bf16[1024,4096]{1,0:T(8,128)(2,1)} custom-call(bf16[1024,2048]{1,0:T(8,128)(2,1)} %emb.1, bf16[4096,2048]{1,0:T(8,128)(2,1)} %cent.1, bf16[1024,4096]{1,0:T(8,128)(2,1)} %grad.1), custom_call_target="tpu_custom_call" | custom-call | tf_op jit(solution)/shard_map/sinkhorn/pallas_call | solution.py:415
  152.9 0.0 copy-done
  152.9 24.5 %convolution_multiply_fusion = f32[4096,2048]{1,0:T(8,128)} fusion(bf16[1024,4096]{1,0:T(8,128)(2,1)} %sinkhorn.1, bf16[1024,2048]{1,0:T(8,128)(2,1)S(1)} %copy-done), kind=kOutput, calls=%fused_computation | convolution fusion | flops 17188257792 | bytes 46137344 | tf_op jit(solution)/shard_map/dot_general | solution.py:434
  177.4 0.0 reduce-scatter.2.cloned.1.call-update
  177.4 23.6 %multiply_convert_fusion = bf16[1024,2048]{1,0:T(8,128)(2,1)} fusion(bf16[1024,4096]{1,0:T(8,128)(2,1)} %sinkhorn.1, bf16[4096,2048]{1,0:T(8,128)(2,1)} %cent.1), kind=kOutput, calls=%fused_computation.1 | convolution fusion | flops 17184063488 | bytes 29360128 | tf_op jit(solution)/shard_map/dot_general | solution.py:438
  201.1 338.8 %reduce-scatter.2.cloned.1.call-done = f32[128,2048]{1,0:T(8,128)} async-done(((f32[4096,2048]{1,0:T(8,128)}), f32[128,2048]{1,0:T(8,128)}) %reduce-scatter.2.cloned.1.call-update) | async-done | bytes 1048592 | tf_op jit(solution)/shard_map/reduce_scatter | solution.py:436
  539.9 2.1 convert_element_type.7
Async XLA Ops:
  7.2 532.8 %reduce-scatter.2.cloned.1.call-start = ((), (), s32[]{:S(2)}) async-start(), calls=%async_computation.1 | async-start | bytes 34603008 | tf_op jit(solution)/shard_map/reduce_scatter | solution.py:436
  7.2 145.7 %copy-start = (bf16[1024,2048]{1,0:T(8,128)(2,1)S(1)}, bf16[1024,2048]{1,0:T(8,128)(2,1)}, u32[]{:S(2)}) copy-start(bf16[1024,2048]{1,0:T(8,128)(2,1)} %emb.1) | copy-start | bytes 12582916
Sparse Core Ops, SparseCore 0:
  177.6 362.3 reduce-scatter.1

commit v2 on v1

--- a/solution.py
+++ b/solution.py
@@ -425,23 +425,238 @@
     )(embeddings, centroids, plan_grad)
 
 
+SUBS = 8
+
+
+def grads_kernel(
+    n, scale, adj_in, emb, cent, eg_out, cg_out,
+    adj, ebuf, embt, cbuf, obuf, own, send, got0, got1, got2, got3, got4,
+    adj_sem, emb_sem, cent_sem, out_sem, ss, rs,
+):
+    gots = (got0, got1, got2, got3, got4)
+    f32, b16 = jnp.float32, jnp.bfloat16
+    rows, C = adj.shape
+    depth = emb.shape[1]
+    sub = depth // SUBS
+    me = lax.axis_index(MESH_AXIS)
+    core = lax.rem(me, 2)
+    mine_q = me // 2
+    nb = len(gots) - 1
+    orders = {0: (0, 1, 2, 3), 1: (1, 0, 2, 3), 2: (2, 3, 0, 1)}
+    kinds = (0, 1, 2, 0, 1, 0, 1, 2)
+
+    def bit(v, b):
+        return lax.rem(v // (1 << b), 2)
+
+    def partner(b):
+        return me + (1 << b) * (1 - 2 * bit(me, b))
+
+    barrier = pltpu.get_barrier_semaphore()
+    for b in range(nb + 1):
+        pl.semaphore_signal(barrier, inc=1, device_id={MESH_AXIS: partner(b)},
+                            device_id_type=pl.DeviceIdType.MESH)
+
+    adj_copy = pltpu.make_async_copy(adj_in, adj, adj_sem)
+    adj_copy.start()
+
+    def emb_copy(c):
+        return pltpu.make_async_copy(
+            emb.at[:, pl.ds(c * 2 * sub, 2 * sub)], ebuf.at[c % 2], emb_sem.at[c % 2])
+
+    def cent_copy(c):
+        return pltpu.make_async_copy(
+            cent.at[:, pl.ds(c * sub, sub)], cbuf.at[c % 2], cent_sem.at[c % 2])
+
+    def out_copy(c):
+        return pltpu.make_async_copy(
+            obuf.at[c % 2], eg_out.at[:, pl.ds(c * sub, sub)], out_sem.at[c % 2])
+
+    heads = n // 2
+
+    def span(l):
+        if l == 0:
+            return (0, heads)
+        size = heads >> l
+        return (heads - 2 * size, size)
+
+    def transfer(s, l):
+        at, size = span(l)
+        b = 0 if l == 0 else orders[kinds[s]][l - 1] + 1
+        return pltpu.make_async_remote_copy(
+            src_ref=send.at[s, pl.ds(at, size)], dst_ref=gots[l].at[s],
+            send_sem=ss.at[s, l], recv_sem=rs.at[s, l],
+            device_id={MESH_AXIS: partner(b)}, device_id_type=pl.DeviceIdType.MESH)
+
+    def level(s, l):
+        order = orders[kinds[s]]
+        transfer(s, l - 1).wait_recv()
+        if l == 1:
+            transfer(s, 0).wait_send()
+        fixed = 0
+        for b in order[:l - 1]:
+            fixed = fixed + (1 << b) * bit(mine_q, b)
+        free = order[l:]
+        here = order[l - 1]
+        mine_bit = bit(mine_q, here)
+        at, size = span(l)
+        got = gots[l - 1]
+
+        @pl.loop(0, size)
+        def _(i):
+            base = fixed
+            for j, b in enumerate(free):
+                base = base + (1 << b) * bit(i, j)
+            away = base + (1 << here) * (1 - mine_bit)
+            keep = base + (1 << here) * mine_bit
+            if l == 1:
+                away_at, keep_at = away, keep
+            else:
+                away_at = 2 * i + 1 - mine_bit
+                keep_at = 2 * i + mine_bit
+            send[s, at + i] = (own[s, away] + got[s, away_at].astype(f32)).astype(b16)
+            own[s, keep] = own[s, keep] + got[s, keep_at].astype(f32)
+
+        transfer(s, l).start()
+
+    def last(s):
+        transfer(s, nb).wait_recv()
+        whole = own[s, mine_q] + gots[nb][s, 0].astype(f32)
+        cg_out[:, s * sub:(s + 1) * sub] = (scale * whole.T).astype(b16)
+
+    group = 4 * LANES
+
+    def partial(c):
+        emb_copy(c).wait()
+        embt[...] = ebuf[c % 2].T
+        if c + 2 < SUBS // 2:
+            emb_copy(c + 2).start()
+
+        @pl.loop(0, C // group)
+        def _(g):
+            res = jnp.dot(embt[...], adj[:, pl.ds(pl.multiple_of(g * group, group), group)],
+                          preferred_element_type=f32)
+            for qq in range(2):
+                r0 = res[:, 2 * qq * LANES:(2 * qq + 1) * LANES]
+                r1 = res[:, (2 * qq + 1) * LANES:(2 * qq + 2) * LANES]
+                kept = jnp.where(core == 0, r0, r1)
+                away = jnp.where(core == 0, r1, r0).astype(b16)
+                for h in range(2):
+                    own[2 * c + h, 2 * g + qq] = kept[h * sub:(h + 1) * sub]
+                    send[2 * c + h, 2 * g + qq] = away[h * sub:(h + 1) * sub]
+
+        if c == 0:
+            pl.semaphore_wait(barrier, nb + 1)
+        transfer(2 * c, 0).start()
+        transfer(2 * c + 1, 0).start()
+
+    block = rows // 2
+
+    def embed(c):
+        cent_copy(c).wait()
+        if c >= 2:
+            out_copy(c - 2).wait()
+
+        @pl.loop(0, rows // block)
+        def _(q):
+            r = pl.ds(pl.multiple_of(q * block, block), block)
+            obuf[c % 2, r, :] = (scale * jnp.dot(
+                adj[r, :], cbuf[c % 2], preferred_element_type=f32)).astype(b16)
+
+        out_copy(c).start()
+        if c + 2 < SUBS:
+            cent_copy(c + 2).start()
+
+    emb_copy(0).start()
+    emb_copy(1).start()
+    cent_copy(0).start()
+    cent_copy(1).start()
+    adj_copy.wait()
+    partial(0)
+    partial(1)
+    level(0, 1)
+    level(1, 1)
+    partial(2)
+    level(2, 1)
+    level(3, 1)
+    partial(3)
+    level(4, 1)
+    level(5, 1)
+    embed(0)
+    level(6, 1)
+    level(7, 1)
+    level(0, 2)
+    level(1, 2)
+    embed(1)
+    level(2, 2)
+    embed(2)
+    level(3, 2)
+    level(4, 2)
+    embed(3)
+    level(0, 3)
+    level(1, 3)
+    embed(4)
+    level(2, 3)
+    level(7, 2)
+    embed(5)
+    level(5, 2)
+    level(6, 2)
+    embed(6)
+    level(3, 3)
+    level(4, 3)
+    level(0, 4)
+    level(1, 4)
+    embed(7)
+    for s, l in ((2, 4), (7, 3), (5, 3), (6, 3), (3, 4), (4, 4), (7, 4), (5, 4), (6, 4)):
+        level(s, l)
+    for s in (0, 1, 2, 3, 4, 7, 5, 6):
+        last(s)
+    for s in range(SUBS):
+        for l in range(1, nb + 1):
+            transfer(s, l).wait_send()
+    out_copy(SUBS - 2).wait()
+    out_copy(SUBS - 1).wait()
+
+
+def grads_of(n, scale, adjoint_b, embeddings, centroids):
+    rows, C = adjoint_b.shape
+    depth = embeddings.shape[1]
+    sub = depth // SUBS
+    heads = n // 2
+    b16, f32 = jnp.bfloat16, jnp.float32
+    vm = pltpu.VMEM
+    dma = pltpu.SemaphoreType.DMA
+    levels = n.bit_length() - 1
+    scratch = [
+        vm((rows, C), b16), vm((2, rows, 2 * sub), b16), vm((2 * sub, rows), b16),
+        vm((2, C, sub), b16), vm((2, rows, sub), b16),
+        vm((SUBS, heads, sub, LANES), f32), vm((SUBS, heads, sub, LANES), b16),
+    ]
+    scratch += [vm((SUBS, heads >> l, sub, LANES), b16) for l in range(levels)]
+    scratch += [dma, dma((2,)), dma((2,)), dma((2,)), dma((SUBS, levels)), dma((SUBS, levels))]
+    return pl.pallas_call(
+        functools.partial(grads_kernel, n, scale),
+        out_shape=(jax.ShapeDtypeStruct((rows, depth), b16),
+                   jax.ShapeDtypeStruct((C // n, depth), b16)),
+        in_specs=[pl.BlockSpec(memory_space=pl.ANY)] * 3,
+        out_specs=(pl.BlockSpec(memory_space=pl.ANY), pl.BlockSpec(memory_space=pltpu.VMEM)),
+        scratch_shapes=scratch,
+        compiler_params=pltpu.CompilerParams(
+            collective_id=1, has_side_effects=True, vmem_limit_bytes=62 * 1024 * 1024),
+        name="grads",
+    )(adjoint_b, embeddings, centroids)
+
+
 def fast_shards(embeddings, centroids, plan_grad):
     n = lax.axis_size("prog")
     rows, depth = embeddings.shape
     scale = 1.0 / (0.25 * depth**0.5)
     ratio = rows * n / centroids.shape[0]
     adjoint_b = adjoint_of(n, scale, ratio, embeddings, centroids, plan_grad)
-    part = scale * lax.dot_general(
-        adjoint_b, embeddings, (((0,), (0,)), ((), ())), preferred_element_type=jnp.float32)
-    centroid_grad = lax.psum_scatter(
-        part, "prog", scatter_dimension=0, tiled=True).astype(jnp.bfloat16)
-    embed_grad = (scale * jnp.dot(
-        adjoint_b, centroids, preferred_element_type=jnp.float32)).astype(jnp.bfloat16)
-    return (embed_grad, centroid_grad)
+    return grads_of(n, scale, adjoint_b, embeddings, centroids)
 
 
 def solution(mesh):
-    fast = mesh.shape["clus"] == 1 and ITERS == 4
+    fast = mesh.shape["clus"] == 1 and mesh.shape["prog"] == 32
     placed = (P("prog", "clus"), P("clus", None), P("prog", "clus"))
     return jax.shard_map(
         fast_shards if fast else general_shards,

time: 549 us -> 251 us (0.46)
  waiting for transfers between devices: 339 us -> 0 us
  Pallas kernels: 146 us -> 244 us
  matrix products: 48.1 us -> 0 us
  between operations: 14.1 us -> 0.65 us
  local copies, waits for them, and re-layouts: 0.01 us -> 5.64 us
    reduce_scatter x1 -> x0, waiting for transfers between devices: 339 us -> none  [fast_shards(): lax.psum_scatter(part, 'prog', scatter_dimension=0, tiled=True)]
    pallas_call x0 -> x1, Pallas kernels: none -> 98.1 us  [grads_of(): pl.pallas_call(functools.partial(grads_kernel, n, scale), out_shape=(jax....]
    dot_general x2 -> x0, matrix products: 48.1 us -> none  [the longest x1 24.5 us: fast_shards(): lax.dot_general(adjoint_b, embeddings, (((0,), (0,)), ((), ())), preferre...]
    unnamed x2 -> x4, local copies, waits for them, and re-layouts: 0.01 us -> 5.64 us
  transfers between devices with their start and end apart: 1 -> 0, of which waited for: 1 -> 0; matrix products, arithmetic and copies ran while one was open for 4% -> 0% of each run, Pallas kernels for 0% -> 0%
where the time goes in v2:
time: 251 us; the launch traced here: 250 us
  Pallas kernels  244 us (97%)
  local copies, waits for them, and re-layouts  5.64 us (2%)
    pallas_call x1, Pallas kernels, adjoint_of(): pl.pallas_call(functools.partial(sinkhorn_kernel, n, scale, ratio), out_s...  146 us
    pallas_call x1, Pallas kernels, grads_of(): pl.pallas_call(functools.partial(grads_kernel, n, scale), out_shape=(jax....  98.1 us
    unnamed x4, local copies, waits for them, and re-layouts  5.64 us

profile of v2, /device:TPU:14, one launch (start us, length us, event | category | flops | bytes accessed | tf_op | source)
XLA Modules:
  0.0 249.9 jit_solution(15781730399111290850)
XLA Ops:
  0.6 145.5 %sinkhorn.1.adj_in = bf16[1024,4096]{1,0:T(8,128)(2,1)} custom-call(bf16[1024,2048]{1,0:T(8,128)(2,1)} %emb.3, bf16[4096,2048]{1,0:T(8,128)(2,1)} %cent.3, bf16[1024,4096]{1,0:T(8,128)(2,1)} %grad.1), custom_call_target="tpu_custom_call" | custom-call | tf_op jit(solution)/shard_map/sinkhorn/pallas_call | solution.py:415
  146.2 98.1 %grads.1 = (bf16[1024,2048]{1,0:T(8,128)(2,1)}, bf16[128,2048]{1,0:T(8,128)(2,1)}) custom-call(bf16[1024,4096]{1,0:T(8,128)(2,1)} %sinkhorn.1.adj_in, bf16[1024,2048]{1,0:T(8,128)(2,1)} %emb.3, bf16[4096,2048]{1,0:T(8,128)(2,1)} %cent.3), custom_call_target="tpu_custom_call" | custom-call | tf_op jit(solution)/shard_map/grads/pallas_call | solution.py:636
  244.2 0.0 copy-start
  244.3 4.8 %copy.7 = bf16[1024,2048]{1,0:T(8,128)(2,1)} copy(bf16[1024,2048]{1,0:T(8,128)(2,1)} %get-tuple-element.4) | data formatting | bytes 8388608
  249.1 0.0 copy-done
  249.1 0.8 copy.8
Async XLA Ops:
  244.2 4.9 %copy-start = (bf16[128,2048]{1,0:T(8,128)(2,1)S(1)}, bf16[128,2048]{1,0:T(8,128)(2,1)}, u32[]{:S(2)}) copy-start(bf16[128,2048]{1,0:T(8,128)(2,1)} %get-tuple-element.5) | copy-start | bytes 1572868
